TPU v7x, 32 devices: a whole 2x2x4 slice. The times are simulated.
32 devices in a mesh: spec: 8 (over z, y), led: 4 (over x, core).
Axes of the slice: x: 2, y: 2, z: 4, core: 2. Of those that a mesh axis runs over, the one named last changes fastest.
Arguments:
- spectrum: float32 [8, 2, 2048, 256], P('spec'), may hold values from -6 to 6
- images: float32 [8, 2, 1024, 1024], P('spec', None, 'led'), may hold values from -6 to 6
- zernike: float32 [8, 16], P('spec'), may hold values from -6 to 6
- pupil_modes: float32 [16, 4, 31], P('led'), may hold values from -0.1875 to 0.1875
- patch_tiles: int32 [8, 25], replicated, may hold values from 0 to 63, as said below
- patch_offsets: int32 [8, 2], replicated, may hold values from 0 to 226
Outputs:
- new_spectrum: float32 [8, 2, 2048, 256], P('spec')
- solve_residual: float32 [8, 2, 2048, 256], P('spec')
Inputs may be any that keep to these rules, and one draw needn't show every extreme that they name: Row l of patch_tiles lists the ids (r + i) * 8 + c + j of a block of 5 x 5 tiles with top left tile (r, c), i and j from 0 to 4, row by row.
All inputs are finite; a program needn't handle non-finite values.
Results may differ from a plain program's by a relative error of at most 0.0003.
Values sent between devices are 32-bit elements; how exact they have to be, the bound alone decides.
A program may use at most 192 MiB of HBM per device.

v0:
```python
import jax
import jax.numpy as jnp
from jax import lax
from jax.sharding import PartitionSpec as P

WIN = 5


damping = 0.5


def toeplitz(kernel, offset, rows_len, cols_len):
    tap_count = kernel.shape[-1]
    distance = (
        jnp.arange(rows_len, dtype=jnp.int32)[:, None]
        - offset
        - jnp.arange(cols_len, dtype=jnp.int32)[None, :]
    )
    matrix = jnp.zeros((2, rows_len, cols_len), kernel.dtype)
    for tap in range(tap_count):
        matrix = matrix + jnp.where(
            distance[None, :, :] == tap, kernel[:, tap][:, None, None], jnp.zeros((), kernel.dtype)
        )
    return matrix


def complex_product(left_side, right_side):
    real_part = jnp.dot(left_side[0], right_side[0], precision=lax.Precision.HIGHEST) - jnp.dot(
        left_side[1], right_side[1], precision=lax.Precision.HIGHEST
    )
    imag_part = jnp.dot(left_side[0], right_side[1], precision=lax.Precision.HIGHEST) + jnp.dot(
        left_side[1], right_side[0], precision=lax.Precision.HIGHEST
    )
    return jnp.stack([real_part, imag_part])


def plain_swap(matrix):
    return jnp.stack([matrix[0].T, matrix[1].T])


def conj_swap(matrix):
    return jnp.stack([matrix[0].T, -matrix[1].T])


def conjugate(matrix):
    return jnp.stack([matrix[0], -matrix[1]])


def forward_cols(window, col_map):
    return complex_product(window, col_map)


def forward_rows(columns, row_map):
    return complex_product(plain_swap(row_map), columns)


def adjoint_rows(picture, row_map):
    return complex_product(conjugate(row_map), picture)


def adjoint_cols(columns, col_map):
    return complex_product(columns, conj_swap(col_map))


def body(spectrum, images, zernike, pupil_modes, patch_tiles, patch_offsets):
    tile_len = spectrum.shape[3]
    row_cells = spectrum.shape[2]
    strip_len = images.shape[2]
    image_len = images.shape[3]
    channel_count = zernike.shape[1]
    tap_count = pupil_modes.shape[2]
    piece_len = strip_len + tap_count - 1
    block_len = WIN * tile_len
    spec_count = lax.axis_size("spec")
    column_here = lax.axis_index("spec")
    strip_here = lax.axis_index("led")
    all_modes = lax.all_gather(pupil_modes, "led", axis=0, tiled=True)
    flat_modes = all_modes.reshape(channel_count, 4 * tap_count)
    own_kernel = jnp.dot(zernike, flat_modes, precision=lax.Precision.HIGHEST).reshape(4, tap_count)
    first_tiles = patch_tiles[:, 0]
    top_tiles = first_tiles // spec_count
    left_tiles = first_tiles % spec_count
    row_starts = top_tiles * tile_len + patch_offsets[:, 0] + strip_here * strip_len
    covered = ((left_tiles <= column_here) & (column_here < left_tiles + WIN)).astype(jnp.float32)
    own_left = jnp.take(left_tiles, column_here)
    own_shift = jnp.take(patch_offsets[:, 1], column_here)
    col_map = toeplitz(own_kernel[0:2], own_shift, block_len, image_len)
    own_column = spectrum[0]
    picture = images[0]

    def cut_pieces(source_column):

        def one_piece(row_start, weight):
            return lax.dynamic_slice_in_dim(source_column, row_start, piece_len, 1) * weight

        return jax.vmap(one_piece)(row_starts, covered)

    def add_pieces(pieces):

        def add_one(position, running):
            row_start = row_starts[position]
            current = lax.dynamic_slice_in_dim(running, row_start, piece_len, 1)
            return lax.dynamic_update_slice_in_dim(
                running, current + pieces[position], row_start, 1
            )

        return lax.fori_loop(
            0, spec_count, add_one, jnp.zeros((2, row_cells, tile_len), jnp.float32)
        )

    def join_block(arriving):
        band_tiles = lax.dynamic_slice_in_dim(arriving, own_left, WIN, 0)
        return band_tiles.transpose(1, 2, 0, 3).reshape(2, band_tiles.shape[2], block_len)

    def part_block(block_cells):
        row_count = block_cells.shape[1]
        pieces_out = block_cells.reshape(2, row_count, WIN, tile_len).transpose(2, 0, 1, 3)
        slots = jnp.zeros((spec_count, 2, row_count, tile_len), jnp.float32)
        return lax.dynamic_update_slice_in_dim(slots, pieces_out, own_left, 0)

    peer_zernike = lax.all_gather(zernike, "spec", axis=0, tiled=True)
    peer_kernels = jnp.dot(peer_zernike, flat_modes, precision=lax.Precision.HIGHEST).reshape(
        spec_count, 4, tap_count
    )
    peer_rows = jax.vmap(lambda kernel: toeplitz(kernel[2:4], 0, piece_len, strip_len))(
        peer_kernels
    )

    def forward(source_column):
        filtered = jax.vmap(forward_rows)(cut_pieces(source_column), peer_rows)
        arriving = lax.all_to_all(filtered, "spec", split_axis=0, concat_axis=0, tiled=True)
        return forward_cols(join_block(arriving), col_map)

    def adjoint(misfit):
        narrowed = adjoint_cols(misfit, col_map)
        returned = lax.all_to_all(
            part_block(narrowed), "spec", split_axis=0, concat_axis=0, tiled=True
        )
        return add_pieces(jax.vmap(adjoint_rows)(returned, peer_rows))

    def fold_terms(contrib):
        return lax.psum(contrib, "led")

    def inner(left_side, right_side):
        return lax.psum(jnp.sum(left_side * right_side), "spec")

    residual = fold_terms(adjoint(picture - forward(own_column))) - damping * own_column
    direction = residual
    norm_now = inner(residual, residual)
    image_dir = fold_terms(adjoint(forward(direction))) + damping * direction
    step_size = norm_now / inner(direction, image_dir)
    update = step_size * direction
    residual = residual - step_size * image_dir
    new_part = own_column + update
    return (new_part[None], residual[None])


def solution(mesh):
    placed = (
        P("spec", None, None, None),
        P("spec", None, "led", None),
        P("spec", None),
        P("led", None, None),
        P(),
        P(),
    )
    return jax.shard_map(
        body,
        mesh=mesh,
        in_specs=placed,
        out_specs=(P("spec", None, None, None), P("spec", None, None, None)),
        check_vma=False,
    )
```

profile of v0, /device:TPU:0, one launch (start us, length us, event | category | flops | bytes accessed | tf_op | source)
XLA Modules:
  0.0 1027.2 jit_solution(9663578451838569944)
XLA Ops:
  13.7 21.3 %all-gather = f32[8,1,16]{2,1,0:T(1,128)S(1)} all-gather(f32[1,1,16]{2,1,0:T(1,128)} %bitcast.295), channel_id=1, replica_groups=mesh['spec'=8,'led'=4] {'spec'}, dimensions={0}, use_global_device_ids=true | all-gather | bytes 576 | tf_op jit(solution)/shard_map/all_gather | solution.py:121
  37.4 8.7 copy.98
  46.2 9.2 gather_fusion
  58.4 14.5 %select_add_fusion.1 = f32[8,2,286,256]{3,2,0,1:T(8,128)S(1)} fusion(f32[8,2]{0,1:T(2,128)S(1)} %get-tuple-element.217, f32[8,2]{0,1:T(2,128)S(1)} %get-tuple-element.218, f32[8,2]{0,1:T(2,128)S(1)} %get-tuple-element.219, f32[8,2]{0,1:T(2,128)S(1)} %get-tuple-element.220, f32[8,2]{0,1:T(2,128)S(1)} %get-tuple-element.221, ...), kind=kLoop, calls=%fused_computation.47 | loop fusion | flops 71458816 | bytes 6957504 | tf_op jit(solution)/shard_map/vmap()/add | solution.py:21
  106.2 28.9 %fusion.30 = (pred[1280,1024]{1,0:T(8,128)(4,1)S(1)}, pred[1280,1024]{1,0:T(8,128)(4,1)S(1)}, pred[1280,1024]{1,0:T(8,128)(4,1)}, pred[1280,1024]{1,0:T(8,128)(4...) fusion(s32[1280]{0:T(1024)S(1)} %iota_subtract_fusion.2), kind=kLoop, calls=%fused_computation.42 | loop fusion | flops 41943040 | bytes 40637440 | tf_op jit(solution)/shard_map/eq | solution.py:22
  135.1 39.8 %select_add_fusion = f32[2,1280,1024]{2,1,0:T(8,128)} fusion(f32[2]{0:T(128)S(1)} %get-tuple-element.248, f32[2]{0:T(128)S(1)} %get-tuple-element.249, f32[2]{0:T(128)S(1)} %get-tuple-element.250, f32[2]{0:T(128)S(1)} %get-tuple-element.251, f32[2]{0:T(128)S(1)} %get-tuple-element.252, f32[2]{0:T(128)S(1)} %get-tuple-element.253, ...), kind=kLoop, calls=%fused_computation.8 | loop fusion | flops 159907840 | bytes 51118328 | tf_op jit(solution)/shard_map/add | solution.py:21
  174.9 17.7 %all-to-all-done = f32[8,2,256,256]{3,2,1,0:T(8,128)} async-done(((f32[8,2,256,256]{3,2,1,0:T(8,128)}), f32[8,2,256,256]{3,2,1,0:T(8,128)}, u32[]{:S(2)}, u32[]{:S(2)}) %all-to-all-start) | async-done | bytes 4194336 | tf_op jit(solution)/shard_map/all_to_all | solution.py:131
  198.4 7.4 fusion.46
  237.2 7.4 fusion.52
  259.3 92.3 %all-to-all-done.1 = f32[8,2,256,256]{3,2,1,0:T(8,128)} async-done(((f32[8,2,256,256]{3,2,1,0:T(8,128)}), f32[8,2,256,256]{3,2,1,0:T(8,128)}, u32[]{:S(2)}, u32[]{:S(2)}) %all-to-all-start.1) | async-done | bytes 4194336 | tf_op jit(solution)/shard_map/all_to_all | solution.py:136
  375.4 49.2 %while.28 = (s32[]{:T(128)}, f32[2,2048,256]{2,0,1:T(2,128)}, s32[8]{0:T(128)S(1)}, f32[8,2,286,256]{3,2,0,1:T(8,128)}, s32[]{:T(128)}, /*index=5*/s32[]{:T(128)}, s32[]{:T(128)}) while((s32[]{:T(128)}, f32[2,2048,256]{2,0,1:T(2,128)}, s32[8]{0:T(128)S(1)}, f32[8,2,286,256]{3,2,0,1:T(8,128)}, s32[]{:T(128)}, /*index=5*/s32[]{:T(128)}, ...), condition=%wide.region_1.2_spmd, body=%wide.region_0.1_spmd.sunk | while | flops 146437 | bytes 4100231 | solution.py:107
  424.6 84.7 %all-reduce.4.cloned.1.call-done = f32[2,2048,256]{2,0,1:T(2,128)} async-done(((f32[2,2048,256]{2,0,1:T(2,128)}), f32[2,2048,256]{2,0,1:T(2,128)}) %all-reduce.4.cloned.1.call-update) | async-done | bytes 4194320 | tf_op jit(solution)/shard_map/psum | solution.py:142
  509.2 9.4 multiply_subtract_fusion
  518.6 9.5 gather_fusion.1
  555.4 98.6 %all_to_all.20 = f32[8,2,256,256]{3,2,1,0:T(8,128)S(1)} all-to-all(f32[8,2,256,256]{3,2,1,0:T(8,128)S(1)} %copy.57), channel_id=1, replica_groups=mesh['spec'=8,'led'=4] {'spec'}, dimensions={0} | all-to-all | bytes 8388608 | tf_op jit(solution)/shard_map/all_to_all | solution.py:131
  658.1 7.0 fusion.40
  665.1 7.4 fusion.42
  699.7 8.7 fusion.54
  725.2 92.3 %all-to-all-done.3 = f32[8,2,256,256]{3,2,1,0:T(8,128)} async-done(((f32[8,2,256,256]{3,2,1,0:T(8,128)}), f32[8,2,256,256]{3,2,1,0:T(8,128)}, u32[]{:S(2)}, u32[]{:S(2)}) %all-to-all-start.3) | async-done | bytes 4194336 | tf_op jit(solution)/shard_map/all_to_all | solution.py:136
  841.5 50.0 %while.29 = (s32[]{:T(128)}, f32[2,2048,256]{2,0,1:T(2,128)}, s32[8]{0:T(128)S(1)}, f32[8,2,286,256]{3,2,0,1:T(8,128)}, s32[]{:T(128)}, /*index=5*/s32[]{:T(128)}, s32[]{:T(128)}) while((s32[]{:T(128)}, f32[2,2048,256]{2,0,1:T(2,128)}, s32[8]{0:T(128)S(1)}, f32[8,2,286,256]{3,2,0,1:T(8,128)}, s32[]{:T(128)}, /*index=5*/s32[]{:T(128)}, ...), condition=%wide.region_6.7_spmd, body=%wide.region_5.6_spmd.sunk | while | flops 146437 | bytes 4100231 | solution.py:107
  891.5 83.8 %all-reduce.6.cloned.1.call-done = f32[2,2048,256]{2,0,1:T(2,128)} async-done(((f32[2,2048,256]{2,0,1:T(2,128)}), f32[2,2048,256]{2,0,1:T(2,128)}) %all-reduce.6.cloned.1.call-update) | async-done | bytes 4194320 | tf_op jit(solution)/shard_map/psum | solution.py:142
  975.4 7.1 multiply_reduce_fusion
  982.4 22.0 %all-reduce = (f32[]{:T(128)}, f32[]{:T(128)}) all-reduce(f32[]{:T(128)} %get-tuple-element.215, f32[]{:T(128)} %get-tuple-element.214), channel_id=1, replica_groups=mesh['spec'=8,'led'=4] {'spec'}, use_global_device_ids=true, to_apply=%region_4.5 | all-reduce | flops 2 | bytes 16 | tf_op jit(solution)/shard_map/psum | solution.py:145
  1005.8 9.5 subtract_bitcast_fusion
  (196 shorter events, 291.8 us)
Async XLA Ops:
  37.4 8.8 copy-start.4
  72.9 16.3 %copy-start.1 = (f32[8,2,286,256]{3,2,0,1:T(8,128)}, f32[8,2,286,256]{3,2,0,1:T(8,128)S(1)}, u32[]{:S(2)}) copy-start(f32[8,2,286,256]{3,2,0,1:T(8,128)S(1)} %select_add_fusion.1) | copy-start | bytes 14057476
  97.6 6.2 copy-start.5
  97.6 95.1 %all-to-all-start = ((f32[8,2,256,256]{3,2,1,0:T(8,128)}), f32[8,2,256,256]{3,2,1,0:T(8,128)}, u32[]{:S(2)}, u32[]{:S(2)}) async-start(f32[8,2,256,256]{3,2,1,0:T(8,128)} %copy.47), calls=%async_computation | async-start | bytes 8388608 | tf_op jit(solution)/shard_map/all_to_all | solution.py:131
  198.2 7.6 copy-start
  215.2 4.9 copy-start.3
  250.1 2.6 copy-start.2
  254.5 97.1 %all-to-all-start.1 = ((f32[8,2,256,256]{3,2,1,0:T(8,128)}), f32[8,2,256,256]{3,2,1,0:T(8,128)}, u32[]{:S(2)}, u32[]{:S(2)}) async-start(f32[8,2,256,256]{3,2,1,0:T(8,128)} %constant_dynamic-update-slice_fusion.1), calls=%async_computation.1 | async-start | bytes 8388608 | tf_op jit(solution)/shard_map/all_to_all | solution.py:136
  259.1 250.2 %all-reduce.4.cloned.1.call-start = ((), (), s32[]{:S(2)}) async-start(), calls=%async_computation.4 | async-start | bytes 8388608 | tf_op jit(solution)/shard_map/psum | solution.py:142
  356.2 9.7 slice-start.3
  361.1 4.8 slice-start.4
  518.6 19.7 %slice-start.5 = ((s8[4718592]{0:T(1024)(128)(4,1)}), s8[524288]{0:T(1024)(128)(4,1)S(1)}, s32[]{:S(2)}) async-start(s8[4718592]{0:T(1024)(128)(4,1)} %bitcast.273), calls=%async_computation.11 | async-start | bytes 1048576
  528.2 10.1 slice-start.6
  657.9 14.7 %slice-start = ((s8[10485760]{0:T(1024)(128)(4,1)}), s8[4194304]{0:T(1024)(128)(4,1)S(1)}, s32[]{:S(2)}) async-start(s8[10485760]{0:T(1024)(128)(4,1)} %bitcast.269), calls=%async_computation.6 | async-start | bytes 8388608
  658.1 14.5 %slice-start.1 = ((s8[10485760]{0:T(1024)(128)(4,1)}), s8[4194304]{0:T(1024)(128)(4,1)S(1)}, s32[]{:S(2)}) async-start(s8[10485760]{0:T(1024)(128)(4,1)} %bitcast.269), calls=%async_computation.7 | async-start | bytes 8388608
  665.1 7.5 slice-start.2
  720.6 96.9 %all-to-all-start.3 = ((f32[8,2,256,256]{3,2,1,0:T(8,128)}), f32[8,2,256,256]{3,2,1,0:T(8,128)}, u32[]{:S(2)}, u32[]{:S(2)}) async-start(f32[8,2,256,256]{3,2,1,0:T(8,128)} %constant_dynamic-update-slice_fusion), calls=%async_computation.3 | async-start | bytes 8388608 | tf_op jit(solution)/shard_map/all_to_all | solution.py:136
  725.2 250.2 %all-reduce.6.cloned.1.call-start = ((), (), s32[]{:S(2)}) async-start(), calls=%async_computation.5 | async-start | bytes 8388608 | tf_op jit(solution)/shard_map/psum | solution.py:142
  822.1 9.7 slice-start.7
  827.0 4.8 slice-start.8
Sparse Core Ops, SparseCore 0:
  424.7 84.4 all-reduce.3
  891.7 83.6 all-reduce.5
where the time goes:
time: 1030 us
  waiting for transfers between devices  371 us (36%)
  matrix products  174 us (17%)
  blocking collectives  148 us (14%)
  other arithmetic  146 us (14%)
  local copies, waits for them, and re-layouts  125 us (12%)
  loops' own time  30.2 us (3%)
  between operations  17.9 us (2%)
  starting transfers between devices  14.3 us (1%)
    all_to_all x2, waiting for transfers between devices, adjoint(): lax.all_to_all(part_block(narrowed), 'spec', split_axis=0, concat_axis=0,...  185 us
    psum x2, waiting for transfers between devices, fold_terms(): return lax.psum(contrib, 'led')  168 us
    all_to_all x1, blocking collectives, forward(): lax.all_to_all(filtered, 'spec', split_axis=0, concat_axis=0, tiled=True)  98.6 us
    add x2, other arithmetic, toeplitz(): matrix + jnp.where(distance[None, :, :] == tap, kernel[:, tap][:, None, N...  54.3 us
    dot_general x8, matrix products, complex_product(): jnp.dot(left_side[1], right_side[0], precision=lax.Precision.HIGHEST)  48.2 us
    dot_general x8, matrix products, complex_product(): jnp.dot(left_side[0], right_side[0], precision=lax.Precision.HIGHEST)  47.5 us
    dot_general x8, matrix products, complex_product(): jnp.dot(left_side[0], right_side[1], precision=lax.Precision.HIGHEST)  39.3 us
    dot_general x8, matrix products, complex_product(): jnp.dot(left_side[1], right_side[1], precision=lax.Precision.HIGHEST)  39 us
  transfers between devices with their start and end apart: 5, of which 5 were waited for; matrix products, arithmetic and copies ran while one was open for 7% of the time, Pallas kernels for 0%

commit v1 on v0

v1 whole, which is shorter than its diff:
```python
import functools

import jax
import jax.numpy as jnp
import numpy as np
from jax import lax
from jax.experimental import pallas as pl
from jax.experimental.pallas import tpu as pltpu
from jax.sharding import PartitionSpec as P

WIN = 5
damping = 0.5
HALO = 64
EDGE = 32
STEP = 192
SPAN = 256
HIGHEST = lax.Precision.HIGHEST


def params(mib, **kw):
    return pltpu.CompilerParams(vmem_limit_bytes=mib * 2**20, **kw)


def split(x):
    high = x.astype(jnp.bfloat16)
    return high, (x - high.astype(jnp.float32)).astype(jnp.bfloat16)


def mm(a, b):
    return jnp.dot(a, b, preferred_element_type=jnp.float32)


def mm3(a_high, a_low, b_high, b_low):
    return mm(a_high, b_high) + mm(a_high, b_low) + mm(a_low, b_high)


def skew(table, shift, width):
    rows, lanes = table.shape
    if width > lanes:
        table = jnp.concatenate([table, jnp.zeros((rows, width - lanes), table.dtype)], axis=1)
    return pltpu.roll(table, shift % width, 1, stride=1, stride_axis=0)


def place_kernel(shift_ref, image_ref, out_ref):
    rows, lanes = image_ref.shape
    slots, _, tile = out_ref.shape
    wide = jnp.concatenate([image_ref[...], jnp.zeros((rows, slots * tile - lanes), jnp.float32)], axis=1)
    wide = pltpu.roll(wide, shift_ref[0], 1)
    for slot in range(slots):
        out_ref[slot] = wide[:, slot * tile : (slot + 1) * tile]


def place(image, shift, slots, tile):
    rows, lanes = image.shape
    step = 64
    return pl.pallas_call(
        place_kernel,
        out_shape=jax.ShapeDtypeStruct((slots, rows, tile), jnp.float32),
        grid_spec=pltpu.PrefetchScalarGridSpec(
            num_scalar_prefetch=1,
            grid=(rows // step,),
            in_specs=[pl.BlockSpec((step, lanes), lambda i, s: (i, 0))],
            out_specs=pl.BlockSpec((slots, step, tile), lambda i, s: (0, i, 0)),
        ),
        compiler_params=params(32),
        name="place",
    )(shift, image)


def back_kernel(base_ref, taps_ref, got_ref, out_ref, acc):
    led = pl.program_id(0)
    _, strip2, tile = got_ref.shape
    strip = strip2 // 2
    quarters, ext, width = out_ref.shape
    own = ext - 2 * EDGE
    tall = strip + 48

    @pl.when(led == 0)
    def _():
        acc[...] = jnp.zeros_like(acc)

    taps = taps_ref[0]
    col = [skew(jnp.broadcast_to(taps[p : p + 1], (tile, 2 * tile)), 0, 2 * tile) for p in (0, 1)]
    cr, ci = col[0], -col[1]
    crm, cim = cr[:, :tile], ci[:, :tile]
    crs, cis = cr[:, tile : tile + HALO], ci[:, tile : tile + HALO]
    top = jnp.concatenate([crm, cim, crs, cis], axis=1)
    low = jnp.concatenate([-cim, crm, -cis, crs], axis=1)
    t_high, t_low = split(jnp.concatenate([top, low], axis=0))
    got = got_ref[0]
    g_high, g_low = split(jnp.concatenate([got[:strip], got[strip:]], axis=1))
    u = mm3(g_high, g_low, t_high, t_low)
    spill = u[:, 2 * tile :]
    lane = lax.broadcasted_iota(jnp.int32, spill.shape, 1)
    turned = pltpu.roll(spill, HALO, 1) * jnp.where(lane < HALO, -1.0, 1.0)
    v = jnp.concatenate([-u[:, tile : 2 * tile], u[:, :tile], turned], axis=1)
    u_high, u_low = split(jnp.concatenate([u, v], axis=0))
    row = [skew(jnp.broadcast_to(taps[p : p + 1, : 2 * strip], (tall, 2 * strip)), -EDGE - 8, 2 * strip)[:, :strip] for p in (2, 3)]
    r_high, r_low = split(jnp.concatenate([row[0], -row[1]], axis=1))
    piece = mm3(r_high, r_low, u_high, u_low)
    base = pl.multiple_of(base_ref[led], 8)
    acc[pl.ds(base, tall), :] += piece

    @pl.when(led == pl.num_programs(0) - 1)
    def _():
        for q in range(quarters):
            out_ref[q] = acc[q * own : q * own + ext, :]


def backproject(got, taps, base, quarters, row_cells):
    leds, strip2, tile = got.shape
    own = row_cells // quarters
    width = 2 * tile + 2 * HALO
    return pl.pallas_call(
        back_kernel,
        out_shape=jax.ShapeDtypeStruct((quarters, own + 2 * EDGE, width), jnp.float32),
        grid_spec=pltpu.PrefetchScalarGridSpec(
            num_scalar_prefetch=1,
            grid=(leds,),
            in_specs=[
                pl.BlockSpec((1, 8, taps.shape[2]), lambda i, s: (i, 0, 0)),
                pl.BlockSpec((1, strip2, tile), lambda i, s: (i, 0, 0)),
            ],
            out_specs=pl.BlockSpec((quarters, own + 2 * EDGE, width), lambda i, s: (0, 0, 0)),
            scratch_shapes=[pltpu.VMEM((row_cells + 2 * EDGE, width), jnp.float32)],
        ),
        compiler_params=params(40),
        name="backproject",
    )(base, taps, got)


def normal_kernel(lead, field_ref, col_ref, row_ref, out_ref, f_high, f_low, u_high, u_low):
    led = pl.program_id(0)
    rows_in, _ = field_ref.shape
    rows_out, wide = out_ref.shape
    tile = wide // 2

    @pl.when(led == 0)
    def _():
        high, low = split(field_ref[...])
        f_high[...] = high
        f_low[...] = low
        out_ref[...] = damping * field_ref[EDGE : EDGE + rows_out, :wide]

    parts = []
    for p in (0, 1):
        table = col_ref[0, p]
        main = skew(table[:tile], -EDGE, 2 * tile)[:, :tile]
        left = skew(table[tile : tile + HALO], -HALO - EDGE, 2 * tile)[:, :tile]
        right = skew(table[tile + HALO :], tile - EDGE, 2 * tile)[:, :tile]
        parts.append((main, jnp.concatenate([left, right], axis=0)))
    (rm, rh), (im, ih) = parts
    matrix = jnp.concatenate(
        [
            jnp.concatenate([rm, im], axis=1),
            jnp.concatenate([-im, rm], axis=1),
            jnp.concatenate([rh, ih], axis=1),
            jnp.concatenate([-ih, rh], axis=1),
        ],
        axis=0,
    )
    m_high, m_low = split(matrix)
    chunk = rows_in // 2
    for k in range(2):
        rows = slice(k * chunk, (k + 1) * chunk)
        u = mm3(f_high[rows, :], f_low[rows, :], m_high, m_low)
        high, low = split(u)
        u_high[rows, :] = high
        u_low[rows, :] = low

    def both(ref, start, size):
        u = ref[start : start + size, :]
        v = jnp.concatenate([-u[:, tile:], u[:, :tile]], axis=1)
        if size < SPAN:
            pad = jnp.zeros((SPAN - size, 2 * tile), u.dtype)
            return jnp.concatenate([u, pad, v, pad], axis=0)
        return jnp.concatenate([u, v], axis=0)

    for start in range(0, rows_out, STEP):
        count = min(STEP, rows_out - start)
        size = min(SPAN, rows_in - start)
        sel = slice(lead + start, lead + start + count)
        pr = skew(row_ref[0, 0, sel, :], 0, SPAN)
        pi = skew(row_ref[0, 1, sel, :], 0, SPAN)
        p_high, p_low = split(jnp.concatenate([pr, -pi], axis=1))
        out_ref[start : start + count, :] += mm3(
            p_high, p_low, both(u_high, start, size), both(u_low, start, size)
        )


def normal(field, col_table, row_table, lead, rows_out):
    rows_in, wide = field.shape
    tile = wide // 3
    leds = col_table.shape[0]
    return pl.pallas_call(
        functools.partial(normal_kernel, lead),
        out_shape=jax.ShapeDtypeStruct((rows_out, 2 * tile), jnp.float32),
        grid=(leds,),
        in_specs=[
            pl.BlockSpec(field.shape, lambda i: (0, 0)),
            pl.BlockSpec((1,) + col_table.shape[1:], lambda i: (i, 0, 0, 0)),
            pl.BlockSpec((1,) + row_table.shape[1:], lambda i: (i, 0, 0, 0)),
        ],
        out_specs=pl.BlockSpec((rows_out, 2 * tile), lambda i: (0, 0)),
        scratch_shapes=[
            pltpu.VMEM((rows_in, wide), jnp.bfloat16),
            pltpu.VMEM((rows_in, wide), jnp.bfloat16),
            pltpu.VMEM((rows_in, 2 * tile), jnp.bfloat16),
            pltpu.VMEM((rows_in, 2 * tile), jnp.bfloat16),
        ],
        compiler_params=params(48),
        name="normal",
        cost_estimate=pl.CostEstimate(
            flops=leds * 2 * 3 * (rows_in * 768 * 512 + rows_out * 512 * 512),
            bytes_accessed=12 * 2**20,
            transcendentals=0,
        ),
    )(field, col_table, row_table)


def body(spectrum, images, zernike, pupil_modes, patch_tiles, patch_offsets):
    tile = spectrum.shape[3]
    row_cells = spectrum.shape[2]
    strip = images.shape[2]
    image_len = images.shape[3]
    channels = zernike.shape[1]
    tap_count = pupil_modes.shape[2]
    reach = tap_count - 1
    spec_count = lax.axis_size("spec")
    led_count = lax.axis_size("led")
    column = lax.axis_index("spec")
    quarter = lax.axis_index("led")
    own = row_cells // led_count
    ext = own + 2 * EDGE

    tops = (patch_tiles[:, 0] // spec_count) * tile + patch_offsets[:, 0]
    lefts = (patch_tiles[:, 0] % spec_count) * tile + patch_offsets[:, 1]

    own_left = lax.dynamic_slice_in_dim(lefts, column, 1)
    slots = place(images.reshape(2 * strip, image_len), own_left, spec_count, tile)
    got = lax.all_to_all(slots, "spec", split_axis=0, concat_axis=0, tiled=True)

    modes = lax.all_gather(pupil_modes, "led", axis=0, tiled=True).reshape(channels, 4 * tap_count)
    coeffs = lax.all_gather(zernike, "spec", axis=0, tiled=True)
    kernels = jnp.dot(coeffs, modes, precision=HIGHEST).reshape(spec_count, 4, tap_count)

    spread = np.zeros((tap_count, tap_count, 128), np.float32)
    for tap in range(tap_count):
        for m in range(2 * tap_count - 1):
            other = tap + m - reach
            if 0 <= other < tap_count:
                spread[other, tap, m + EDGE - reach] = 1.0
    shifted = jnp.einsum("lqo,otm->lqtm", kernels, jnp.asarray(spread), precision=HIGHEST)

    def products(re, im):
        kr, ki = kernels[:, re, :, None], kernels[:, im, :, None]
        sr, si = shifted[:, re], shifted[:, im]
        return jnp.stack([kr * sr + ki * si, ki * sr - kr * si], axis=1)

    def band(cells, starts, prods):
        tap = jnp.arange(tap_count, dtype=jnp.int32)[None, None, :]
        gap = cells[None, :, None] - starts[:, None, None]
        inside = ((tap <= gap) & (tap > gap - image_len)).astype(jnp.float32)
        return jnp.einsum("lxt,lptm->lpxm", inside, prods, precision=HIGHEST)

    col_cells = column * tile + jnp.concatenate(
        [
            jnp.arange(tile, dtype=jnp.int32),
            jnp.arange(-HALO, 0, dtype=jnp.int32),
            jnp.arange(tile, tile + HALO, dtype=jnp.int32),
        ]
    )
    row_cells_here = quarter * own - EDGE + jnp.arange(ext, dtype=jnp.int32)
    col_table = band(col_cells, lefts, products(0, 1))
    row_table = band(row_cells_here, tops, products(2, 3))

    first = tops + quarter * strip + EDGE
    base = first // 8 * 8
    lane = jnp.arange(2 * tile, dtype=jnp.int32)[None, None, :]
    tap = jnp.arange(tap_count, dtype=jnp.int32)[None, :, None]
    late = EDGE + 8 - (first - base)
    backward = (lane == late[:, None, None] - tap).astype(jnp.float32)
    back = jnp.einsum("lpt,ltj->lpj", kernels[:, 2:4], backward, precision=HIGHEST)
    onward = jnp.pad(kernels[:, 0:2], ((0, 0), (0, 0), (0, 2 * tile - tap_count)))
    taps = jnp.pad(jnp.concatenate([onward, back], axis=1), ((0, 0), (0, 4), (0, 0)))

    to_right = [(i, i + 1) for i in range(spec_count - 1)]
    to_left = [(i + 1, i) for i in range(spec_count - 1)]

    def pack(parts):
        return jnp.concatenate([parts[0], parts[1]], axis=1)

    padded = jnp.pad(spectrum[0], ((0, 0), (2 * EDGE, 2 * EDGE), (0, 0)))
    here = lax.dynamic_slice_in_dim(padded, quarter * own, own + 4 * EDGE, 1)
    from_left = lax.ppermute(here[:, :, tile - HALO :], "spec", to_right)
    from_right = lax.ppermute(here[:, :, :HALO], "spec", to_left)
    field = jnp.concatenate(
        [here[0], here[1], from_left[0], from_right[0], from_left[1], from_right[1]], axis=1
    )
    modelled = normal(field, col_table, row_table, 0, ext)

    partial = backproject(got, taps, base, led_count, row_cells)
    summed = lax.psum_scatter(partial, "led", scatter_dimension=0, tiled=False)

    rough = summed[:, : 2 * tile] - modelled
    spill = summed[:, 2 * tile :]
    rr, ri = rough[:, :tile], rough[:, tile:]
    rightward = jnp.concatenate([rr[:, tile - HALO :], ri[:, tile - HALO :], spill], axis=1)
    leftward = jnp.concatenate([rr[:, :HALO], ri[:, :HALO]], axis=1)
    left_in = lax.ppermute(rightward, "spec", to_right)
    right_in = lax.ppermute(leftward, "spec", to_left) + spill
    spill_in = left_in[:, 2 * HALO :]
    start_r = rr[:, :HALO] + spill_in[:, :HALO]
    start_i = ri[:, :HALO] + spill_in[:, HALO:]
    residual_ext = jnp.concatenate(
        [
            start_r,
            rr[:, HALO:],
            start_i,
            ri[:, HALO:],
            left_in[:, :HALO],
            right_in[:, :HALO],
            left_in[:, HALO : 2 * HALO],
            right_in[:, HALO:],
        ],
        axis=1,
    )
    residual_own = residual_ext[EDGE : EDGE + own, : 2 * tile]
    residual_all = lax.all_gather(residual_own, "led", axis=0, tiled=True)
    image_own = normal(residual_ext, col_table, row_table, EDGE, own)
    sums = jnp.stack([jnp.sum(residual_own * residual_own), jnp.sum(residual_own * image_own)])
    totals = lax.psum(sums, ("spec", "led"))
    image_all = lax.all_gather(image_own, "led", axis=0, tiled=True)
    step_size = totals[0] / totals[1]

    def unpack(packed):
        return jnp.stack([packed[:, :tile], packed[:, tile:]])

    final = unpack(residual_all)
    return (
        (spectrum[0] + step_size * final)[None],
        (final - step_size * unpack(image_all))[None],
    )


def solution(mesh):
    placed = (
        P("spec", None, None, None),
        P("spec", None, "led", None),
        P("spec", None),
        P("led", None, None),
        P(),
        P(),
    )
    return jax.shard_map(
        body,
        mesh=mesh,
        in_specs=placed,
        out_specs=(P("spec", None, None, None), P("spec", None, None, None)),
        check_vma=False,
    )
```

time: 1030 us -> 349 us (0.34)
  waiting for transfers between devices: 371 us -> 62.4 us
  matrix products: 174 us -> 8.48 us
  other arithmetic: 146 us -> 13.9 us
  local copies, waits for them, and re-layouts: 125 us -> 33.5 us
  Pallas kernels: 0 us -> 65.8 us
  loops' own time: 30.2 us -> 0 us
  blocking collectives: 148 us -> 123 us
  starting transfers between devices: 14.3 us -> 25.1 us
    all_to_all x3 -> x1, waiting for transfers between devices: 202 us -> 9.48 us  [body(): got = lax.all_to_all(slots, 'spec', split_axis=0, concat_axis=0, tiled=True)]
    psum x2 -> x0, waiting for transfers between devices: 168 us -> none  [fold_terms(): return lax.psum(contrib, 'led')]
    dot_general x34 -> x5, matrix products: 174 us -> 8.48 us  [the longest x2 7.43 us: band(): return jnp.einsum('lxt,lptm->lpxm', inside, prods, precision=HIGHEST)]
    all_to_all x1 -> x0, blocking collectives: 98.6 us -> none  [forward(): lax.all_to_all(filtered, 'spec', split_axis=0, concat_axis=0, tiled=True)]
    add x19 -> x5, other arithmetic: 72.7 us -> 1.29 us  [the longest x1 1 us: body(): right_in = lax.ppermute(leftward, 'spec', to_left) + spill]
    pallas_call x0 -> x4, Pallas kernels: none -> 65.8 us  [the longest x2 46.4 us: normal(): pl.pallas_call(functools.partial(normal_kernel, lead), out_shape=jax.Shap...]
    all_gather x2, blocking collectives: 27.7 us -> 82.9 us  [the longest x1 77.7 us: body(): coeffs = lax.all_gather(zernike, 'spec', axis=0, tiled=True)]
    dynamic_slice x34 -> x1, local copies, waits for them, and re-layouts: 35.4 us -> 0.59 us  [body(): own_left = lax.dynamic_slice_in_dim(lefts, column, 1)]
  transfers between devices with their start and end apart: 5 -> 8, of which waited for: 5 -> 6; matrix products, arithmetic and copies ran while one was open for 7% -> 8% of each run, Pallas kernels for 0% -> 7%
where the time goes in v1:
time: 349 us; the launch traced here: 348 us
  blocking collectives  123 us (35%)
  Pallas kernels  65.8 us (19%)
  waiting for transfers between devices  62.4 us (18%)
  local copies, waits for them, and re-layouts  33.5 us (10%)
  starting transfers between devices  25.1 us (7%)
  between operations  15.3 us (4%)
  other arithmetic  13.9 us (4%)
  matrix products  8.48 us (2%)
    all_gather x1, blocking collectives, body(): coeffs = lax.all_gather(zernike, 'spec', axis=0, tiled=True)  77.7 us
    pallas_call x2, Pallas kernels, normal(): pl.pallas_call(functools.partial(normal_kernel, lead), out_shape=jax.Shap...  46.4 us
    psum x1, blocking collectives, body(): totals = lax.psum(sums, ('spec', 'led'))  40.5 us
    all_gather x1, waiting for transfers between devices, body(): image_all = lax.all_gather(image_own, 'led', axis=0, tiled=True)  23 us
    pallas_call x1, Pallas kernels, backproject(): pl.pallas_call(back_kernel, out_shape=jax.ShapeDtypeStruct((quarters, own...  16.6 us
    unnamed x27, local copies, waits for them, and re-layouts  11.3 us
    reduce_scatter x1, waiting for transfers between devices, body(): summed = lax.psum_scatter(partial, 'led', scatter_dimension=0, tiled=False)  10.7 us
    ppermute x1, starting transfers between devices, body(): from_left = lax.ppermute(here[:, :, tile - HALO:], 'spec', to_right)  10.3 us
  transfers between devices with their start and end apart: 8, of which 6 were waited for; matrix products, arithmetic and copies ran while one was open for 8% of the time, Pallas kernels for 7%

profile of v1, /device:TPU:0, one launch (start us, length us, event | category | flops | bytes accessed | tf_op | source)
XLA Modules:
  0.0 347.9 jit_solution(16924686593150463935)
XLA Ops:
  10.9 2.7 place.1
  15.7 7.4 %all-to-all-start = ((f32[8,512,256]{2,1,0:T(8,128)}), f32[8,512,256]{2,1,0:T(8,128)}, u32[]{:S(2)}, u32[]{:S(2)}) async-start(f32[8,512,256]{2,1,0:T(8,128)} %copy-done.1), calls=%async_computation | async-start | bytes 8388608 | tf_op jit(solution)/shard_map/all_to_all | solution.py:241
  23.2 5.2 %all_gather.13 = f32[16,4,31]{2,1,0:T(4,128)S(1)} all-gather(f32[4,4,31]{2,1,0:T(4,128)S(1)} %copy-done.9), channel_id=1, replica_groups=mesh['spec'=8,'led'=4] {'led'}, dimensions={0}, use_global_device_ids=true | all-gather | bytes 9920 | tf_op jit(solution)/shard_map/all_gather | solution.py:243
  28.5 77.7 %all-gather = f32[8,1,16]{2,1,0:T(1,128)S(1)} all-gather(f32[1,1,16]{2,1,0:T(1,128)S(1)} %bitcast.74), channel_id=1, replica_groups=mesh['spec'=8,'led'=4] {'spec'}, dimensions={0}, use_global_device_ids=true | all-gather | bytes 576 | tf_op jit(solution)/shard_map/all_gather | solution.py:244
  106.9 9.5 %all-to-all-done.got_ref = f32[8,512,256]{2,1,0:T(8,128)} async-done(((f32[8,512,256]{2,1,0:T(8,128)}), f32[8,512,256]{2,1,0:T(8,128)}, u32[]{:S(2)}, u32[]{:S(2)}) %all-to-all-start) | async-done | bytes 4194336 | tf_op jit(solution)/shard_map/all_to_all | solution.py:241
  116.4 16.6 %backproject.1 = f32[4,576,640]{2,1,0:T(8,128)S(1)} custom-call(s32[8]{0:T(128)S(1)} %get-tuple-element.6.base_ref, f32[8,8,512]{2,1,0:T(8,128)S(1)} %pad.13.taps_ref, f32[8,512,256]{2,1,0:T(8,128)} %all-to-all-done.got_ref), custom_call_target="tpu_custom_call" | custom-call | tf_op jit(solution)/shard_map/backproject/pallas_call | solution.py:114
  133.0 2.5 copy-done
  137.4 10.3 %collective-permute-start = (f32[2,640,64]{1,2,0:T(8,128)S(1)}, f32[2,640,64]{1,2,0:T(8,128)S(1)}, u32[]{:S(2)}, u32[]{:S(2)}) collective-permute-start(f32[2,640,64]{1,2,0:T(8,128)S(1)} %copy.31), channel_id=1, source_target_pairs={{0,4},{4,8},{8,12},{12,16},{16,20},{20,24},{24,28},{1,5},{5,9},{9,... | collective-permute-start | bytes 983048 | tf_op jit(solution)/shard_map/ppermute | solution.py:295
  150.8 4.3 %convolution_bitcast_fusion.row_ref = f32[8,2,576,128]{3,2,1,0:T(8,128)} fusion(s32[8,576]{1,0:T(8,128)S(1)} %get-tuple-element.51, s32[8,576]{1,0:T(8,128)S(1)} %get-tuple-element.50, f32[8,2,31,128]{3,0,2,1:T(8,128)S(1)} %get-tuple-element.58), kind=kOutput, calls=%fused_computation.8 | convolution fusion | flops 439257600 | bytes 5009408 | tf_op jit(solution)/shard_map/lxt,lptm->lpxm/dot_general | solution.py:264
  155.2 3.1 convolution_bitcast_fusion.1.col_ref
  161.5 3.0 concatenate.47.field_ref
  164.5 23.9 %normal.2 = f32[576,512]{1,0:T(8,128)S(1)} custom-call(f32[640,768]{1,0:T(8,128)S(1)} %concatenate.47.field_ref, f32[8,2,384,128]{3,2,1,0:T(8,128)} %convolution_bitcast_fusion.1.col_ref, f32[8,2,576,128]{3,2,1,0:T(8,128)} %convolution_bitcast_fusion.row_ref), custom_call_target="tpu_custom_call" | custom-call | flops 19327352832 | bytes 12582912 | tf_op jit(solution)/shard_map/normal/pallas_call | solution.py:195
  188.4 10.7 %reduce-scatter.2.cloned.1.call-done = f32[1,576,640]{2,1,0:T(8,128)} async-done(((f32[4,576,640]{2,1,0:T(8,128)}), f32[1,576,640]{2,1,0:T(8,128)}) %reduce-scatter.2.cloned.1.call-update) | async-done | bytes 1474576 | tf_op jit(solution)/shard_map/reduce_scatter | solution.py:303
  202.3 9.3 %collective-permute-done.3 = f32[576,128]{1,0:T(8,128)S(1)} collective-permute-done((f32[576,128]{1,0:T(8,128)S(1)}, f32[576,128]{1,0:T(8,128)S(1)}, u32[]{:S(2)}, u32[]{:S(2)}) %collective-permute-start.3) | collective-permute-done | bytes 294944 | tf_op jit(solution)/shard_map/ppermute | solution.py:311
  212.8 4.5 %collective-permute-start.2 = (f32[576,256]{1,0:T(8,128)S(1)}, f32[576,256]{1,0:T(8,128)S(1)}, u32[]{:S(2)}, u32[]{:S(2)}) collective-permute-start(f32[576,256]{1,0:T(8,128)S(1)} %pad_maximum_fusion.4), channel_id=1, source_target_pairs={{0,4},{4,8},{8,12},{12,16},{16,20},{20,24},{24,28},{1,5},{5,9},{9,... | collective-permute-start | bytes 1769480 | tf_op jit(solution)/shard_map/ppermute | solution.py:310
  219.7 9.1 %collective-permute-done.2 = f32[576,256]{1,0:T(8,128)S(1)} collective-permute-done((f32[576,256]{1,0:T(8,128)S(1)}, f32[576,256]{1,0:T(8,128)S(1)}, u32[]{:S(2)}, u32[]{:S(2)}) %collective-permute-start.2) | collective-permute-done | bytes 589856 | tf_op jit(solution)/shard_map/ppermute | solution.py:310
  229.9 4.2 %concatenate.52.field_ref = f32[576,768]{1,0:T(8,128)} concatenate(f32[576,64]{1,0:T(8,128)S(1)} %get-tuple-element.30, f32[576,192]{1,0:T(8,128)} %get-tuple-element.27, f32[576,64]{1,0:T(8,128)} %get-tuple-element.31, f32[576,192]{1,0:T(8,128)} %get-tuple-element.26, f32[576,64]{1,0:T(8,128)} %get-tuple-element.29, f32[576,64]{1,0:T(8,128)} %get-tuple-element.43, ...), dimensions={1} | concatenate | bytes 3538944 | tf_op jit(solution)/shard_map/concatenate | solution.py:315
  235.5 22.5 %normal.3 = f32[512,512]{1,0:T(8,128)} custom-call(f32[576,768]{1,0:T(8,128)S(1)} %copy-done.4, f32[8,2,384,128]{3,2,1,0:T(8,128)S(1)} %copy-done.2, f32[8,2,576,128]{3,2,1,0:T(8,128)} %convolution_bitcast_fusion.row_ref), custom_call_target="tpu_custom_call" | custom-call | flops 17314086912 | bytes 12582912 | tf_op jit(solution)/shard_map/normal/pallas_call | solution.py:195
  258.0 3.6 %multiply_reduce_fusion.1 = (f32[]{:T(128)}, f32[]{:T(128)}, f32[512,512]{1,0:T(8,128)}) fusion(f32[512,512]{1,0:T(8,128)} %normal.3, f32[576,192]{1,0:T(8,128)} %get-tuple-element.26, f32[576,64]{1,0:T(8,128)} %get-tuple-element.31, f32[576,192]{1,0:T(8,128)} %get-tuple-element.27, f32[576,64]{1,0:T(8,128)S(1)} %get-tuple-element.30), kind=kLoop, calls=%fused_computation.19 | loop fusion | flops 1835006 | bytes 3276808 | tf_op jit(solution)/shard_map/reduce_sum | solution.py:331
  263.7 40.5 %psum.7 = f32[2]{0:T(128)S(1)} all-reduce(f32[2]{0:T(128)S(1)} %pad_maximum_fusion.8), channel_id=1, replica_groups=mesh['spec'=8,'led'=4] {'spec','led'}, use_global_device_ids=true, to_apply=%region_3.4 | all-reduce | flops 2 | bytes 16 | tf_op jit(solution)/shard_map/psum | solution.py:332
  306.1 4.4 %slice_bitcast_fusion.3 = (f32[1,1,2048,256]{3,2,1,0:T(8,128)S(1)}, f32[1,1,2048,256]{3,2,1,0:T(8,128)}) fusion(f32[2048,512]{1,0:T(8,128)} %all-gather.4.cloned.1.call-done), kind=kLoop, calls=%fused_computation.12 | loop fusion | bytes 8388608 | tf_op jit(solution)/shard_map/stack | solution.py:337
  310.5 23.0 %all-gather.6.cloned.1.call-done = f32[2048,512]{1,0:T(8,128)} async-done(((f32[512,512]{1,0:T(8,128)}), f32[2048,512]{1,0:T(8,128)}) %all-gather.6.cloned.1.call-update) | async-done | bytes 4194320 | tf_op jit(solution)/shard_map/all_gather | solution.py:333
  333.6 2.7 slice_bitcast_fusion.1
  337.7 3.7 %fusion = (f32[1,2,2048,256]{3,2,1,0:T(8,128)}, f32[1,2,2048,256]{3,2,1,0:T(8,128)}) fusion(f32[1,1,2048,256]{3,2,1,0:T(8,128)S(1)} %get-tuple-element.11, f32[1,1,2048,256]{3,2,1,0:T(8,128)S(1)} %get-tuple-element.10, f32[1,1,2048,256]{3,2,1,0:T(8,128)S(1)} %copy-done.7, f32[1,1,2048,256]{3,2,1,0:T(8,128)S(1)} %get-tuple-element.12, f32[]{:T(128)} %bitcast.30, ...), kind=kLoop, calls=%fused_computation.2 | loop fusion | flops 6291456 | bytes 20971524 | tf_op jit(solution)/shard_map/sub | solution.py:342
  (78 shorter events, 28.1 us)
Async XLA Ops:
  9.3 1.6 copy-start.3
  13.7 2.0 copy-start.1
  15.7 7.5 %copy-start.9 = (f32[4,4,31]{2,1,0:T(4,128)S(1)}, f32[4,4,31]{2,1,0:T(4,128)}, u32[]{:S(2)}) copy-start(f32[4,4,31]{2,1,0:T(4,128)} %param.10) | copy-start | bytes 5956
  15.7 12.8 %copy-start.10 = (f32[1,16]{1,0:T(1,128)S(1)}, f32[1,16]{1,0:T(1,128)}, u32[]{:S(2)}) copy-start(f32[1,16]{1,0:T(1,128)} %param.9) | copy-start | bytes 196
  15.7 100.7 %all-to-all-start = ((f32[8,512,256]{2,1,0:T(8,128)}), f32[8,512,256]{2,1,0:T(8,128)}, u32[]{:S(2)}, u32[]{:S(2)}) async-start(f32[8,512,256]{2,1,0:T(8,128)} %copy-done.1), calls=%async_computation | async-start | bytes 8388608 | tf_op jit(solution)/shard_map/all_to_all | solution.py:241
  23.1 176.0 %reduce-scatter.2.cloned.1.call-start = ((), (), s32[]{:S(2)}) async-start(), calls=%async_computation.2 | async-start | bytes 7372800 | tf_op jit(solution)/shard_map/reduce_scatter | solution.py:303
  133.0 2.5 copy-start
  135.6 14.3 %copy-start.8 = (f32[31,31,128,1]{2,0,1,3:T(8,128)S(1)}, f32[31,31,128,1]{2,0,1,3:T(8,128)}, u32[]{:S(2)}) copy-start(f32[31,31,128,1]{2,0,1,3:T(8,128)} %constant.85) | copy-start | bytes 1476100
  135.6 170.5 %all-gather.4.cloned.1.call-start = ((), (), s32[]{:S(2)}) async-start(), calls=%async_computation.3 | async-start | bytes 5242880 | tf_op jit(solution)/shard_map/all_gather | solution.py:329
  137.4 21.8 %collective-permute-start = (f32[2,640,64]{1,2,0:T(8,128)S(1)}, f32[2,640,64]{1,2,0:T(8,128)S(1)}, u32[]{:S(2)}, u32[]{:S(2)}) collective-permute-start(f32[2,640,64]{1,2,0:T(8,128)S(1)} %copy.31), channel_id=1, source_target_pairs={{0,4},{4,8},{8,12},{12,16},{16,20},{20,24},{24,28},{1,5},{5,9},{9,... | collective-permute-start | bytes 983048 | tf_op jit(solution)/shard_map/ppermute | solution.py:295
  147.9 11.7 %collective-permute-start.1 = (f32[2,640,64]{1,2,0:T(8,128)S(1)}, f32[2,640,64]{1,2,0:T(8,128)S(1)}, u32[]{:S(2)}, u32[]{:S(2)}) collective-permute-start(f32[2,640,64]{1,2,0:T(8,128)S(1)} %copy.33), channel_id=1, source_target_pairs={{4,0},{8,4},{12,8},{16,12},{20,16},{24,20},{28,24},{5,1},{9,5},{13... | collective-permute-start | bytes 983048 | tf_op jit(solution)/shard_map/ppermute | solution.py:296
  150.8 7.4 %copy-start.5 = (f32[1,2,2048,256]{3,2,1,0:T(8,128)S(1)}, f32[1,2,2048,256]{3,2,1,0:T(8,128)}, u32[]{:S(2)}) copy-start(f32[1,2,2048,256]{3,2,1,0:T(8,128)} %param.7) | copy-start | bytes 12582916
  201.0 10.6 %collective-permute-start.3 = (f32[576,128]{1,0:T(8,128)S(1)}, f32[576,128]{1,0:T(8,128)S(1)}, u32[]{:S(2)}, u32[]{:S(2)}) collective-permute-start(f32[576,128]{1,0:T(8,128)S(1)} %pad_maximum_fusion.5), channel_id=1, source_target_pairs={{4,0},{8,4},{12,8},{16,12},{20,16},{24,20},{28,24},{5,1},{9,5},{13... | collective-permute-start | bytes 884744 | tf_op jit(solution)/shard_map/ppermute | solution.py:311
  212.8 16.0 %collective-permute-start.2 = (f32[576,256]{1,0:T(8,128)S(1)}, f32[576,256]{1,0:T(8,128)S(1)}, u32[]{:S(2)}, u32[]{:S(2)}) collective-permute-start(f32[576,256]{1,0:T(8,128)S(1)} %pad_maximum_fusion.4), channel_id=1, source_target_pairs={{0,4},{4,8},{8,12},{12,16},{16,20},{20,24},{24,28},{1,5},{5,9},{9,... | collective-permute-start | bytes 1769480 | tf_op jit(solution)/shard_map/ppermute | solution.py:310
  218.8 15.3 %copy-start.2 = (f32[8,2,384,128]{3,2,1,0:T(8,128)S(1)}, f32[8,2,384,128]{3,2,1,0:T(8,128)}, u32[]{:S(2)}) copy-start(f32[8,2,384,128]{3,2,1,0:T(8,128)} %convolution_bitcast_fusion.1.col_ref) | copy-start | bytes 9437188
  234.1 1.5 copy-start.4
  261.6 71.9 %all-gather.6.cloned.1.call-start = ((), (), s32[]{:S(2)}) async-start(), calls=%async_computation.4 | async-start | bytes 5242880 | tf_op jit(solution)/shard_map/all_gather | solution.py:333
  333.5 3.4 copy-start.6
  333.5 4.1 %copy-start.7 = (f32[1,1,2048,256]{3,2,1,0:T(8,128)S(1)}, f32[1,1,2048,256]{3,2,1,0:T(8,128)}, u32[]{:S(2)}) copy-start(f32[1,1,2048,256]{3,2,1,0:T(8,128)} %get-tuple-element.13) | copy-start | bytes 6291460
Sparse Core Ops, SparseCore 0:
  135.7 63.3 reduce-scatter.1
  261.8 35.1 all-gather.3
  299.2 34.2 all-gather.5
